TPU v7x, 256 devices: a whole 4x4x8 slice. The times are simulated.
256 devices in a mesh: dp: 64 (over z, y, core), proto: 4 (over x).
Axes of the slice: x: 4, y: 4, z: 8, core: 2. Of those that a mesh axis runs over, the one named last changes fastest.
Arguments:
- student_feat: bfloat16 [16384, 256], P('dp'), may hold values from -6 to 6
- teacher_feat: bfloat16 [16384, 256], P('dp'), may hold values from -6 to 6
- prototypes: bfloat16 [65536, 256], P(('dp', 'proto')), may hold values from -6 to 6
Outputs:
- grad_student: float32 [16384, 256], P('dp')
- grad_proto: float32 [65536, 256], P(('dp', 'proto'))
All inputs are finite; a program needn't handle non-finite values.
Results may differ from a plain program's by a relative error of at most 0.0041.
Values may be sent and summed in bfloat16 or wider, within the bound.
A program may use at most 128 MiB of HBM per device.

v0:
```python
import jax
import jax.numpy as jnp
from jax import lax
from jax.sharding import PartitionSpec as P

SWEEPS = 3


teacher_temp = 0.07
student_temp = 0.1
loss_scale = 1024.0
epsilon = 1e-06


def unit_rows(matrix):
    values = matrix.astype(jnp.float32)
    inverse = lax.rsqrt(jnp.sum(values * values, axis=-1, keepdims=True) + epsilon)
    return (values * inverse, inverse)


def shards(student_feat, teacher_feat, prototypes):
    contract = (((1,), (1,)), ((), ()))
    student_unit, student_inverse = unit_rows(student_feat)
    student_bf = student_unit.astype(jnp.bfloat16)
    teacher_unit, teacher_inverse = unit_rows(teacher_feat)
    teacher_bf = teacher_unit.astype(jnp.bfloat16)
    gathered = lax.all_gather(prototypes, "dp", axis=0, tiled=True)
    gathered_unit, gathered_inverse = unit_rows(gathered)
    gathered_bf = gathered_unit.astype(jnp.bfloat16)
    crops_all = student_feat.shape[0] * lax.axis_size("dp")
    protos_all = gathered.shape[0] * lax.axis_size("proto")
    teacher_exp = jnp.exp(
        lax.dot_general(teacher_bf, gathered_bf, contract, preferred_element_type=jnp.float32)
        / teacher_temp
    )
    student_exp = jnp.exp(
        lax.dot_general(student_bf, gathered_bf, contract, preferred_element_type=jnp.float32)
        / student_temp
    )
    partition_local = jnp.sum(student_exp, axis=1)
    row_scale = jnp.ones((student_feat.shape[0],), jnp.float32)
    col_scale = jnp.ones((gathered.shape[0],), jnp.float32)
    for sweep_index in range(SWEEPS):
        col_local = jnp.dot(row_scale, teacher_exp, precision=lax.Precision.HIGHEST)
        col_total = lax.psum(col_local, "dp")
        col_scale = 1.0 / (protos_all * col_total)
        row_local = jnp.dot(teacher_exp, col_scale, precision=lax.Precision.HIGHEST)
        row_total = lax.psum(row_local, "proto")
        row_scale = 1.0 / (crops_all * row_total)
    partition = lax.psum(partition_local, "proto")
    targets = crops_all * teacher_exp * row_scale[:, None] * col_scale[None, :]
    logit_grad = (loss_scale * (student_exp / partition[:, None] - targets) / student_temp).astype(
        jnp.bfloat16
    )
    unit_part = jnp.dot(logit_grad, gathered_bf, preferred_element_type=jnp.float32)
    unit_grad = lax.psum(unit_part, "proto")
    grad_student = student_inverse * (
        unit_grad - student_unit * jnp.sum(student_unit * unit_grad, axis=1, keepdims=True)
    )
    proto_unit_grad = lax.psum_scatter(
        lax.dot_general(
            logit_grad, student_bf, (((0,), (0,)), ((), ())), preferred_element_type=jnp.float32
        ),
        "dp",
        scatter_dimension=0,
        tiled=True,
    )
    own_unit, own_inverse = unit_rows(prototypes)
    grad_proto = own_inverse * (
        proto_unit_grad - own_unit * jnp.sum(own_unit * proto_unit_grad, axis=1, keepdims=True)
    )
    return (grad_student, grad_proto)


def solution(mesh):
    in_specs = (P("dp", None), P("dp", None), P(("dp", "proto"), None))
    out_specs = (P("dp", None), P(("dp", "proto"), None))
    return jax.shard_map(shards, mesh=mesh, in_specs=in_specs, out_specs=out_specs, check_vma=False)
```

profile of v0, /device:TPU:32, one launch (start us, length us, event | category | flops | bytes accessed | tf_op | source)
XLA Modules:
  0.0 988.2 jit_solution(16883993083641745392)
XLA Ops:
  7.2 0.0 all-gather.2.cloned.1.call-start
  7.2 0.7 all-gather.2.cloned.1.call-update
  7.9 0.0 all-reduce.6.cloned.1.call-start
  7.9 1.0 fusion.16
  9.0 87.6 %all-gather.2.cloned.1.call-done = bf16[16384,256]{1,0:T(8,128)(2,1)} async-done(((bf16[256,256]{1,0:T(8,128)(2,1)}), bf16[16384,256]{1,0:T(8,128)(2,1)}) %all-gather.2.cloned.1.call-update) | async-done | bytes 8388624 | tf_op jit(solution)/shard_map/all_gather | solution.py:27
  96.6 5.2 fusion.2
  101.9 0.0 copy-start.2
  101.9 6.7 fusion
  108.6 0.0 copy-start
  108.6 5.7 copy-done
  114.3 8.6 fusion.24
  122.9 0.0 all-reduce.6.cloned.1.call-update
  122.9 0.2 all-reduce.8.cloned.1.call-start
  123.2 0.1 fusion.15
  123.3 163.1 %all-reduce.6.cloned.1.call-done = f32[16384]{0:T(1024)} async-done(((f32[16384]{0:T(1024)}), f32[16384]{0:T(1024)}) %all-reduce.6.cloned.1.call-update) | async-done | bytes 65552 | tf_op jit(solution)/shard_map/psum | solution.py:45
  286.4 0.9 multiply_divide_fusion.2
  287.3 16.1 %fusion.32 = f32[1,256]{1,0:T(1,128)S(1)} fusion(f32[256,16384]{1,0:T(8,128)} %copy-done, f32[16384,1]{0,1:T(1,128)S(1)} %bitcast.28), kind=kOutput, calls=%fused_computation.47 | convolution fusion | flops 50331648 | bytes 16843776 | tf_op jit(solution)/shard_map/dot_general | solution.py:47
  303.3 10.4 %psum.58 = f32[256]{0:T(256)S(1)} all-reduce(f32[256]{0:T(256)S(1)} %bitcast.31), channel_id=1, replica_groups=mesh['dp'=64,'proto'=4] {'proto'}, use_global_device_ids=true, to_apply=%region_6.0 | all-reduce | flops 256 | bytes 2048 | tf_op jit(solution)/shard_map/psum | solution.py:48
  313.7 12.1 %fusion.33 = f32[1,16384]{1,0:T(1,128)} fusion(f32[256,1]{0,1:T(1,128)S(1)} %bitcast.32, f32[256,16384]{1,0:T(8,128)} %copy-done), kind=kOutput, calls=%fused_computation.48 | convolution fusion | flops 50331648 | bytes 16843776 | tf_op jit(solution)/shard_map/dot_general | solution.py:44
  325.8 0.0 all-reduce.8.cloned.1.call-update
  325.8 0.0 all-reduce.10.cloned.1.call-start
  325.9 162.9 %all-reduce.8.cloned.1.call-done = f32[16384]{0:T(1024)} async-done(((f32[16384]{0:T(1024)}), f32[16384]{0:T(1024)}) %all-reduce.8.cloned.1.call-update) | async-done | bytes 65552 | tf_op jit(solution)/shard_map/psum | solution.py:45
  488.8 0.9 multiply_divide_fusion.1
  489.6 16.1 %fusion.34 = f32[1,256]{1,0:T(1,128)S(1)} fusion(f32[256,16384]{1,0:T(8,128)} %copy-done, f32[16384,1]{0,1:T(1,128)S(1)} %bitcast.29), kind=kOutput, calls=%fused_computation.49 | convolution fusion | flops 50331648 | bytes 16843776 | tf_op jit(solution)/shard_map/dot_general | solution.py:47
  505.7 10.6 %psum.60 = f32[256]{0:T(256)S(1)} all-reduce(f32[256]{0:T(256)S(1)} %bitcast.33), channel_id=1, replica_groups=mesh['dp'=64,'proto'=4] {'proto'}, use_global_device_ids=true, to_apply=%region_8.0 | all-reduce | flops 256 | bytes 2048 | tf_op jit(solution)/shard_map/psum | solution.py:48
  516.3 12.1 %fusion.35 = f32[1,16384]{1,0:T(1,128)} fusion(f32[256,1]{0,1:T(1,128)S(1)} %bitcast.34, f32[256,16384]{1,0:T(8,128)} %copy-done), kind=kOutput, calls=%fused_computation.50 | convolution fusion | flops 50331648 | bytes 16843776 | tf_op jit(solution)/shard_map/dot_general | solution.py:44
  528.4 0.0 all-reduce.10.cloned.1.call-update
  528.4 0.0 all-reduce.12.cloned.1.call-start
  528.5 13.6 %fusion.31 = (f32[256]{0:T(256)S(1)}, f32[256,16384]{1,0:T(8,128)}) fusion(bf16[16384,256]{1,0:T(8,128)(2,1)} %all-gather.2.cloned.1.call-done, f32[16384]{0:T(1024)S(1)} %add_rsqrt_fusion, bf16[256,256]{1,0:T(8,128)(2,1)S(1)} %copy-done.2, f32[256]{0:T(256)S(1)} %add_rsqrt_fusion.3), kind=kOutput, calls=%fused_computation.46 | convolution fusion | flops 2168651520 | bytes 25364480 | tf_op jit(solution)/shard_map/dot_general | solution.py:37
  542.1 149.3 %all-reduce.10.cloned.1.call-done = f32[16384]{0:T(1024)} async-done(((f32[16384]{0:T(1024)}), f32[16384]{0:T(1024)}) %all-reduce.10.cloned.1.call-update) | async-done | bytes 65552 | tf_op jit(solution)/shard_map/psum | solution.py:45
  691.4 0.9 multiply_divide_fusion
  692.2 16.1 %fusion.36 = f32[1,256]{1,0:T(1,128)S(1)} fusion(f32[256,16384]{1,0:T(8,128)} %copy-done, f32[16384,1]{0,1:T(1,128)S(1)} %bitcast.24), kind=kOutput, calls=%fused_computation.51 | convolution fusion | flops 50331648 | bytes 16843776 | tf_op jit(solution)/shard_map/dot_general | solution.py:47
  708.3 10.7 %all-reduce = (f32[256]{0:T(256)S(1)}, f32[256]{0:T(256)S(1)}) all-reduce(f32[256]{0:T(256)S(1)} %bitcast.30, f32[256]{0:T(256)S(1)} %get-tuple-element.4), channel_id=1, replica_groups=mesh['dp'=64,'proto'=4] {'proto'}, use_global_device_ids=true, to_apply=%region_10.0 | all-reduce | flops 512 | bytes 4096 | tf_op jit(solution)/shard_map/psum | solution.py:48
  719.0 11.7 %multiply_convert_fusion = bf16[256,16384]{1,0:T(8,128)(2,1)S(1)} fusion(f32[256,16384]{1,0:T(8,128)} %copy-done, f32[256,16384]{1,0:T(8,128)} %get-tuple-element.5, f32[16384]{0:T(1024)S(1)} %multiply_divide_fusion, f32[256]{0:T(256)S(1)} %divide_multiply_fusion, f32[256]{0:T(256)S(1)} %get-tuple-element.3), kind=kLoop, calls=%fused_computation.8 | loop fusion | flops 25165824 | bytes 42010624 | tf_op jit(solution)/shard_map/convert_element_type | solution.py:52
  730.7 3.2 copy-done.1
  733.9 6.7 fusion.27
  740.6 0.0 all-reduce.12.cloned.1.call-update
  740.7 0.0 copy-start.3
  740.7 0.0 reduce-scatter.2.cloned.1.call-start
  740.7 11.6 %fusion.21 = f32[16384,256]{1,0:T(8,128)} fusion(bf16[256,16384]{1,0:T(8,128)(2,1)} %copy-done.1, bf16[256,256]{1,0:T(8,128)(2,1)S(1)} %copy-done.2, f32[256]{0:T(256)S(1)} %add_rsqrt_fusion.3), kind=kOutput, calls=%fused_computation.35 | convolution fusion | flops 2147680256 | bytes 25297920 | tf_op jit(solution)/shard_map/dot_general | solution.py:61
  752.3 0.0 reduce-scatter.2.cloned.1.call-update
  752.4 0.1 fusion.18
  752.5 31.5 %all-reduce.12.cloned.1.call-done = f32[256,256]{1,0:T(8,128)} async-done(((f32[256,256]{1,0:T(8,128)}), f32[256,256]{1,0:T(8,128)}) %all-reduce.12.cloned.1.call-update) | async-done | bytes 262160 | tf_op jit(solution)/shard_map/psum | solution.py:56
  784.0 1.1 fusion.12
  785.1 1.8 fusion.14
  786.9 191.0 %reduce-scatter.2.cloned.1.call-done = f32[256,256]{1,0:T(8,128)} async-done(((f32[16384,256]{1,0:T(8,128)}), f32[256,256]{1,0:T(8,128)}) %reduce-scatter.2.cloned.1.call-update) | async-done | bytes 262160 | tf_op jit(solution)/shard_map/reduce_scatter | solution.py:60
  977.9 1.1 fusion.9
  979.1 1.8 fusion.11
  (10 shorter events, 0.1 us)
Async XLA Ops:
  7.2 89.4 %all-gather.2.cloned.1.call-start = ((), (), s32[]{:S(2)}) async-start(), calls=%async_computation.1 | async-start | bytes 8519680 | tf_op jit(solution)/shard_map/all_gather | solution.py:27
  7.9 278.5 %all-reduce.6.cloned.1.call-start = ((), (), s32[]{:S(2)}) async-start(), calls=%async_computation.2 | async-start | bytes 131072 | tf_op jit(solution)/shard_map/psum | solution.py:45
  101.9 21.3 %copy-start.2 = (bf16[256,256]{1,0:T(8,128)(2,1)S(1)}, bf16[256,256]{1,0:T(8,128)(2,1)}, u32[]{:S(2)}) copy-start(bf16[256,256]{1,0:T(8,128)(2,1)} %param.3) | copy-start | bytes 393220
  108.6 5.7 copy-start
  122.9 365.8 %all-reduce.8.cloned.1.call-start = ((), (), s32[]{:S(2)}) async-start(), calls=%async_computation.3 | async-start | bytes 131072 | tf_op jit(solution)/shard_map/psum | solution.py:45
  325.8 365.5 %all-reduce.10.cloned.1.call-start = ((), (), s32[]{:S(2)}) async-start(), calls=%async_computation.4 | async-start | bytes 131072 | tf_op jit(solution)/shard_map/psum | solution.py:45
  528.4 255.6 %all-reduce.12.cloned.1.call-start = ((), (), s32[]{:S(2)}) async-start(), calls=%async_computation.5 | async-start | bytes 524288 | tf_op jit(solution)/shard_map/psum | solution.py:56
  730.7 3.2 copy-start.1
  740.7 11.7 %copy-start.3 = (bf16[256,256]{1,0:T(8,128)(2,1)S(1)}, bf16[256,256]{1,0:T(8,128)(2,1)}, u32[]{:S(2)}) copy-start(bf16[256,256]{1,0:T(8,128)(2,1)} %param.5) | copy-start | bytes 393220
  740.7 237.3 %reduce-scatter.2.cloned.1.call-start = ((), (), s32[]{:S(2)}) async-start(), calls=%async_computation.6 | async-start | bytes 17039360 | tf_op jit(solution)/shard_map/reduce_scatter | solution.py:60
Sparse Core Ops, SparseCore 0:
  10.8 85.7 all-gather.1
  123.0 163.2 all-reduce.5
  326.0 162.7 all-reduce.7
  528.5 162.7 all-reduce.9
  740.8 43.1 all-reduce.11
  789.0 188.9 reduce-scatter.1
where the time goes:
time: 997 us; the launch traced here: 988 us
  waiting for transfers between devices  786 us (79%)
  matrix products  120 us (12%)
  blocking collectives  31.7 us (3%)
  other arithmetic  26.7 us (3%)
  between operations  14.7 us (1%)
    psum x3, waiting for transfers between devices, shards(): col_total = lax.psum(col_local, 'dp')  475 us
    reduce_scatter x1, waiting for transfers between devices, shards(): lax.psum_scatter(lax.dot_general(logit_grad, student_bf, (((0,), (0,)), (...  191 us
    all_gather x1, waiting for transfers between devices, shards(): gathered = lax.all_gather(prototypes, 'dp', axis=0, tiled=True)  87.6 us
    dot_general x3, matrix products, shards(): row_local = jnp.dot(teacher_exp, col_scale, precision=lax.Precision.HIGHEST)  48.2 us
    dot_general x3, matrix products, shards(): col_local = jnp.dot(row_scale, teacher_exp, precision=lax.Precision.HIGHEST)  32.7 us
    psum x3, blocking collectives, shards(): row_total = lax.psum(row_local, 'proto')  31.7 us
    psum x1, waiting for transfers between devices, shards(): unit_grad = lax.psum(unit_part, 'proto')  31.5 us
  transfers between devices with their start and end apart: 6, of which 6 were waited for; matrix products, arithmetic and copies ran while one was open for 3% of the time, Pallas kernels for 0%

commit v1 on v0

v1 whole, which is shorter than its diff:
```python
import functools
import math

import jax
import jax.numpy as jnp
from jax import lax
from jax.experimental import pallas as pl
from jax.experimental.pallas import tpu as pltpu
from jax.sharding import PartitionSpec as P

NZ, NY, NX, NC = 8, 4, 4, 2
B = 256
ROWS = NY * NC * B
COLS = NZ * B
CROPS = 16384
PROTOS = 65536
SWEEPS = 3
teacher_temp = 0.07
student_temp = 0.1
loss_scale = 1024.0
epsilon = 1e-06
LOG2E = math.log2(math.e)
MESH = pl.DeviceIdType.MESH
NT = (((1,), (1,)), ((), ()))
f32 = jnp.float32
bf16 = jnp.bfloat16
SUB = 4
PIECE = B // SUB
TILE = 512


def unit_rows(matrix):
    values = matrix.astype(f32)
    inverse = lax.rsqrt(jnp.sum(values * values, axis=-1, keepdims=True) + epsilon)
    return values * inverse, inverse


def kernel(
    student_ref, teacher_ref, proto_ref, gs_ref, gp_ref,
    protos, teach, stud, stud_t, t_exp, s_exp, grad, part, row_a, row_b, mat,
    col_send, col_recv, row_sib, row_send, sib_recv, row_recv,
    chunk, ring_send, ring_recv, u_ref, u_send, u_sib, v_send, v_recv, q_send, q_full,
    ag_ss, ag_rs, cr_ss, cr_rs, fw_ss, fw_rs, col_ss, col_rs, sib_ss, sib_rs, row_ss, row_rs,
    rg_ss, rg_rs, us_ss, us_rs, v_ss, v_rs, q_ss, q_rs,
):
    dp = lax.axis_index("dp")
    x = lax.axis_index("proto")
    z, y, c = dp // (NY * NC), (dp // NC) % NY, dp % NC

    def dev(dz, dy, flip, dx):
        core = 1 - c if flip else c
        return ((((z + dz) % NZ) * NY + (y + dy) % NY) * NC + core, (x + dx) % NX)

    right, left, sibling = dev(1, 0, 0, 0), dev(NZ - 1, 0, 0, 0), dev(0, 0, 1, 0)
    z_peers = [(o, dev(o, 0, 0, 0)) for o in range(1, NZ)]
    yx_peers = [((a, b), dev(0, a, 0, b)) for a in range(NY) for b in range(NX) if (a, b) != (0, 0)]

    def copy(src, dst, ss, rs, to):
        return pltpu.make_async_remote_copy(
            src_ref=src, dst_ref=dst, send_sem=ss, recv_sem=rs, device_id=to, device_id_type=MESH
        )

    barrier = pltpu.get_barrier_semaphore()
    for _, peer in z_peers + yx_peers:
        pl.semaphore_signal(barrier, inc=1, device_id=peer, device_id_type=MESH)
    pl.semaphore_signal(barrier, inc=1, device_id=sibling, device_id_type=MESH)

    protos[0:B, :] = unit_rows(proto_ref[...])[0].astype(bf16)
    teach[0:B, :] = unit_rows(teacher_ref[...])[0].astype(bf16)
    stud[0:B, :] = unit_rows(student_ref[...])[0].astype(bf16)
    pl.semaphore_wait(barrier, len(z_peers) + len(yx_peers) + 1)

    sent = []

    ag = {}

    def ag_step(k):
        for s in range(SUB):
            for d in (0, 1):
                if k == 3 and (2 * s) // SUB != d:
                    continue
                if k > 0:
                    ag[(k - 1, s, d)].wait_recv()
                src = (NZ - k) % NZ if d == 0 else k
                dst = NZ - k - 1 if d == 0 else k + 1
                cp = copy(
                    protos.at[pl.ds(src * B + s * PIECE, PIECE)],
                    protos.at[pl.ds(dst * B + s * PIECE, PIECE)],
                    ag_ss.at[k, s, d], ag_rs.at[k, s, d], right if d == 0 else left,
                )
                cp.start()
                ag[(k, s, d)] = cp
                sent.append(cp)

    def ag_wait(k):
        for s in range(SUB):
            for d in (0, 1):
                cp = ag.get((k, s, d))
                if cp is not None:
                    cp.wait_recv()

    cr, fw = {}, {}

    def crop_send(w, ref):
        for j in (1, 3, 2):
            t = (NY - j) % NY
            cp = copy(
                ref.at[pl.ds(0, B)], ref.at[pl.ds(2 * t * B, B)],
                cr_ss.at[w, j - 1], cr_rs.at[w, t - 1], dev(0, j, 0, 0),
            )
            cp.start()
            cr[(w, j)] = cp
            sent.append(cp)
        forward(w, ref, 0)

    def forward(w, ref, j):
        cp = copy(
            ref.at[pl.ds(2 * j * B, B)], ref.at[pl.ds((2 * j + 1) * B, B)],
            fw_ss.at[w, j], fw_rs.at[w, j], sibling,
        )
        cp.start()
        fw[(w, j)] = cp
        sent.append(cp)

    def crop_forward(w, ref):
        for j in (1, 3, 2):
            cr[(w, (NY - j) % NY)].wait_recv()
            forward(w, ref, j)

    def crop_wait(w):
        for j in range(NY):
            fw[(w, j)].wait_recv()

    lane_tiles = COLS // 128

    def teacher_slot(s):
        weights = protos[s * B:(s + 1) * B, :]

        def body(i, acc):
            rows = pl.ds(pl.multiple_of(i * TILE, TILE), TILE)
            dots = lax.dot_general(teach[rows, :], weights, NT, preferred_element_type=f32)
            values = jnp.exp2(dots * (LOG2E / teacher_temp))
            t_exp[rows, s * B:(s + 1) * B] = values
            return acc + jnp.sum(values.reshape(TILE // 8, 8, B), axis=0)

        acc = lax.fori_loop(0, ROWS // TILE, body, jnp.zeros((8, B), f32))
        col_send[0, s:s + 1, :] = jnp.sum(acc, axis=0, keepdims=True)

    def student_slot(s):
        weights = protos[s * B:(s + 1) * B, :]

        def body(i, _):
            rows = pl.ds(pl.multiple_of(i * TILE, TILE), TILE)
            dots = lax.dot_general(stud[rows, :], weights, NT, preferred_element_type=f32)
            values = jnp.exp2(dots * (LOG2E / student_temp))
            s_exp[rows, s * B:(s + 1) * B] = values
            both = values[:, :128] + values[:, 128:]
            part[rows, :] = both if s == 0 else part[rows, :] + both
            return 0

        lax.fori_loop(0, ROWS // TILE, body, 0)

    ag_step(0)
    crop_send(0, teach)
    crop_send(1, stud)
    ag_step(1)
    crop_forward(0, teach)
    ag_step(2)
    crop_wait(0)
    teacher_slot(0)
    teacher_slot(1)
    teacher_slot(7)
    ag_step(3)
    crop_forward(1, stud)
    teacher_slot(2)
    teacher_slot(6)
    for s in range(SUB):
        ag[(2, s, 1 - (2 * s) // SUB)].wait_recv()
    teacher_slot(3)
    teacher_slot(5)
    ag_wait(3)
    teacher_slot(4)
    crop_wait(1)

    def start_col(n):
        cps = []
        for o, peer in z_peers:
            t = (NZ - o) % NZ
            cp = copy(col_send.at[n], col_recv.at[n, t - 1], col_ss.at[n, o - 1], col_rs.at[n, t - 1], peer)
            cp.start()
            cps.append(cp)
        sent.extend(cps)
        return cps

    def finish_col(n, cps):
        total = col_send[n]
        for cp in cps:
            cp.wait_recv()
        for o in range(1, NZ):
            total = total + pltpu.roll(col_recv[n, o - 1], o, 0)
        return 1.0 / (PROTOS * total)

    def start_sibling(n, height):
        cp = copy(
            row_sib.at[n, pl.ds(0, height)], sib_recv.at[n, pl.ds(0, height)],
            sib_ss.at[n], sib_rs.at[n], sibling,
        )
        cp.start()
        sent.append(cp)
        return cp

    even = lax.broadcasted_iota(jnp.int32, (8, B), 0) % 2 == 0

    def swap(v):
        return jnp.where(even, pltpu.roll(v, 7, 0), pltpu.roll(v, 1, 0))

    def start_row(n, height, cp):
        cp.wait_recv()
        for h in range(0, height, 8):
            row_send[n, h:h + 8, :] = row_sib[n, h:h + 8, :] + swap(sib_recv[n, h:h + 8, :])
        cps = []
        for (a, b), peer in yx_peers:
            i, t = a * NX + b, ((NY - a) % NY) * NX + (NX - b) % NX
            cp = copy(
                row_send.at[n, pl.ds(0, height)], row_recv.at[n, t - 1, pl.ds(0, height)],
                row_ss.at[n, i - 1], row_rs.at[n, t - 1], peer,
            )
            cp.start()
            cps.append(cp)
        sent.extend(cps)
        return cps

    def finish_row(n, height, cps):
        for cp in cps:
            cp.wait_recv()
        out = []
        for h in range(0, height, 8):
            total = row_send[n, h:h + 8, :]
            for a in range(NY):
                some = None
                for b in range(NX):
                    if (a, b) == (0, 0):
                        continue
                    v = row_recv[n, a * NX + b - 1, h:h + 8, :]
                    some = v if some is None else some + v
                total = total + (some if a == 0 else pltpu.roll(some, 2 * a, 0))
            out.append(total)
        return out

    lane = lax.broadcasted_iota(jnp.int32, (B, 128), 1)

    def to_lanes(n, h):
        row_sib[n, h:h + 8, :] = jnp.transpose(mat[...])[0:8, :]

    def to_rows(v, out):
        wide = jnp.transpose(jnp.concatenate([v, jnp.zeros((120, B), f32)], axis=0))
        for q in range(8):
            out[q * B:(q + 1) * B, :] = jnp.broadcast_to(wide[:, q:q + 1], (B, 128))

    def row_pass(col):
        mat[...] = jnp.zeros((B, 128), f32)

        def body(q, _):
            rows = pl.ds(pl.multiple_of(q * B, B), B)
            acc = jnp.zeros((B, 128), f32)
            for t in range(lane_tiles):
                s, h = t // 2, t % 2
                acc = acc + t_exp[rows, t * 128:(t + 1) * 128] * col[s:s + 1, h * 128:(h + 1) * 128]
            mat[...] = jnp.where(lane == q, jnp.sum(acc, axis=1, keepdims=True), mat[...])
            return 0

        lax.fori_loop(0, 8, body, 0)

    def partition_pass():
        mat[...] = jnp.zeros((B, 128), f32)

        def body(q, _):
            rows = pl.ds(pl.multiple_of(q * B, B), B)
            mat[...] = jnp.where(lane == q, jnp.sum(part[rows, :], axis=1, keepdims=True), mat[...])
            return 0

        lax.fori_loop(0, 8, body, 0)

    def col_pass(n):
        def body(i, acc):
            rows = pl.ds(pl.multiple_of(i * 64, 64), 64)
            scale = jnp.concatenate([row_b[rows, :]] * lane_tiles, axis=1)
            values = t_exp[rows, :] * scale
            return acc + jnp.sum(values.reshape(8, 8, COLS), axis=0)

        acc = lax.fori_loop(0, ROWS // 64, body, jnp.zeros((8, COLS), f32))
        total = jnp.sum(acc, axis=0, keepdims=True)
        for s in range(NZ):
            col_send[n, s:s + 1, :] = total[:, s * B:(s + 1) * B]

    cps = start_col(0)
    for s in range(4):
        student_slot(s)
    col = finish_col(0, cps)
    row_pass(col)
    to_lanes(0, 0)
    cps = start_row(0, 8, start_sibling(0, 8))
    for s in range(4, 8):
        student_slot(s)
    (row_total,) = finish_row(0, 8, cps)
    to_rows(1.0 / (CROPS * row_total), row_b)
    col_pass(1)
    cps = start_col(1)
    partition_pass()
    to_lanes(1, 8)
    for q in range(8):
        stud_t[:, q * B:(q + 1) * B] = jnp.transpose(stud[q * B:(q + 1) * B, :].astype(f32)).astype(bf16)
    col = finish_col(1, cps)
    row_pass(col)
    to_lanes(1, 0)
    cps = start_row(1, 16, start_sibling(1, 16))
    row_total, partition = finish_row(1, 16, cps)
    to_rows(1.0 / (CROPS * row_total), row_b)
    col_pass(2)
    cps = start_col(2)
    to_rows((loss_scale / student_temp) / partition, row_a)
    col = finish_col(2, cps)
    row_pass(col)
    to_lanes(2, 0)
    cps = start_row(2, 8, start_sibling(2, 8))
    (row_total,) = finish_row(2, 8, cps)
    to_rows((loss_scale / student_temp) / row_total, row_b)

    def grad_slot(s):
        cols = slice(s * B, (s + 1) * B)

        def body(i, _):
            rows = pl.ds(pl.multiple_of(i * B, B), B)
            a = row_a[rows, :]
            b = row_b[rows, :]
            for h in range(2):
                at = slice(s * B + h * 128, s * B + (h + 1) * 128)
                scale = col[s:s + 1, h * 128:(h + 1) * 128]
                grad[rows, at] = (s_exp[rows, at] * a - t_exp[rows, at] * b * scale).astype(bf16)
            return 0

        lax.fori_loop(0, ROWS // B, body, 0)
        chunk[s] = jnp.dot(stud_t[...], grad[:, cols], preferred_element_type=f32)

    rg = {}
    H = B // 2

    def ring(m, d, h):
        s = 4 - m if d == 0 else 4 + m
        rows = slice(h * H, (h + 1) * H)
        value = chunk[s, rows, :]
        if (m - 1, d, h) in rg:
            rg[(m - 1, d, h)].wait_recv()
            value = value + ring_recv[m - 1, d, rows, :].astype(f32)
        ring_send[m, d, rows, :] = value.astype(bf16)
        cp = copy(
            ring_send.at[m, d, pl.ds(h * H, H)], ring_recv.at[m, d, pl.ds(h * H, H)],
            rg_ss.at[m, d, h], rg_rs.at[m, d, h], right if d == 0 else left,
        )
        cp.start()
        rg[(m, d, h)] = cp
        sent.append(cp)

    def u_block(q):
        return jnp.dot(grad[q * B:(q + 1) * B, :], protos[...], preferred_element_type=f32)

    grad_slot(4)
    ring(0, 0, 0)
    ring(0, 1, 1)
    grad_slot(3)
    ring(1, 0, 1)
    grad_slot(5)
    ring(1, 1, 0)
    grad_slot(2)
    grad_slot(6)
    ring(1, 0, 0)
    ring(1, 1, 1)
    grad_slot(1)
    grad_slot(7)
    ring(2, 0, 1)
    ring(2, 1, 0)
    grad_slot(0)
    us = []
    for j in range(NY):
        u_send[j] = u_block(2 * j + 1).astype(bf16)
        cp = copy(u_send.at[j], u_sib.at[j], us_ss.at[j], us_rs.at[j], sibling)
        cp.start()
        us.append(cp)
    sent.extend(us)
    ring(2, 0, 0)
    ring(2, 1, 1)
    for j in range(NY):
        u_ref[j] = u_block(2 * j)
    for j in range(NY):
        us[j].wait_recv()
        total = u_ref[j] + u_sib[j].astype(f32)
        u_ref[j] = total
        v_send[j] = total.astype(bf16)
    Q = B // NX
    vs = []
    for (a, b), peer in yx_peers:
        i, t = a * NX + b, ((NY - a) % NY) * NX + (NX - b) % NX
        at = pl.multiple_of(((x + b) % NX) * Q, Q)
        cp = copy(v_send.at[a, pl.ds(at, Q)], v_recv.at[t - 1], v_ss.at[i - 1], v_rs.at[t - 1], peer)
        cp.start()
        vs.append(cp)
    sent.extend(vs)
    ring(3, 0, 1)
    ring(3, 1, 0)
    ring(3, 0, 0)
    ring(3, 1, 1)

    mine = pl.ds(pl.multiple_of(x * Q, Q), Q)
    for cp in vs:
        cp.wait_recv()
    total = u_ref[0, mine, :]
    for i in range(NY * NX - 1):
        total = total + v_recv[i].astype(f32)
    unit, inverse = unit_rows(student_ref[mine, :])
    q_send[...] = inverse * (total - unit * jnp.sum(unit * total, axis=1, keepdims=True))
    qs = []
    for b in range(1, NX):
        t = NX - b
        cp = copy(q_send, q_full.at[pl.ds(pl.multiple_of(x * Q, Q), Q)], q_ss.at[b - 1], q_rs.at[t - 1], dev(0, 0, 0, b))
        cp.start()
        qs.append(cp)
    sent.extend(qs)

    for key in ((3, 0, 1), (3, 1, 0), (3, 0, 0), (3, 1, 1)):
        rg[key].wait_recv()
    total = chunk[0] + ring_recv[3, 0].astype(f32) + ring_recv[3, 1].astype(f32)
    total = jnp.transpose(total)
    unit, inverse = unit_rows(proto_ref[...])
    gp_ref[...] = inverse * (total - unit * jnp.sum(unit * total, axis=1, keepdims=True))

    for cp in qs:
        cp.wait_recv()
    gs_ref[...] = q_full[...]
    gs_ref[mine, :] = q_send[...]
    for cp in sent:
        cp.wait_send()


def shards(student_feat, teacher_feat, prototypes):
    vmem = pltpu.VMEM
    dma = pltpu.SemaphoreType.DMA
    n_yx = NY * NX - 1
    pairs = [
        dma((4, SUB, 2)), dma((2, NY - 1)), dma((2, NY)), dma((SWEEPS, NZ - 1)), dma((SWEEPS,)),
        dma((SWEEPS, n_yx)), dma((4, 2, 2)), dma((NY,)), dma((n_yx,)), dma((NX - 1,)),
    ]
    return pl.pallas_call(
        kernel,
        out_shape=[jax.ShapeDtypeStruct((B, B), f32), jax.ShapeDtypeStruct((B, B), f32)],
        in_specs=[pl.BlockSpec(memory_space=pltpu.VMEM)] * 3,
        out_specs=[pl.BlockSpec(memory_space=pltpu.VMEM)] * 2,
        scratch_shapes=[
            vmem((COLS, B), bf16),
            vmem((ROWS, B), bf16),
            vmem((ROWS, B), bf16),
            vmem((B, ROWS), bf16),
            vmem((ROWS, COLS), f32),
            vmem((ROWS, COLS), f32),
            vmem((ROWS, COLS), bf16),
            vmem((ROWS, 128), f32),
            vmem((ROWS, 128), f32),
            vmem((ROWS, 128), f32),
            vmem((B, 128), f32),
            vmem((SWEEPS, 8, B), f32),
            vmem((SWEEPS, NZ - 1, 8, B), f32),
            vmem((SWEEPS, 16, B), f32),
            vmem((SWEEPS, 16, B), f32),
            vmem((SWEEPS, 16, B), f32),
            vmem((SWEEPS, n_yx, 16, B), f32),
            vmem((NZ, B, B), f32),
            vmem((4, 2, B, B), bf16),
            vmem((4, 2, B, B), bf16),
            vmem((NY, B, B), f32),
            vmem((NY, B, B), bf16),
            vmem((NY, B, B), bf16),
            vmem((NY, B, B), bf16),
            vmem((n_yx, B // NX, B), bf16),
            vmem((B // NX, B), f32),
            vmem((B, B), f32),
        ] + [s for s in pairs for _ in range(2)],
        compiler_params=pltpu.CompilerParams(
            collective_id=0, has_side_effects=True, vmem_limit_bytes=63 * 2**20
        ),
    )(student_feat, teacher_feat, prototypes)


def solution(mesh):
    in_specs = (P("dp", None), P("dp", None), P(("dp", "proto"), None))
    out_specs = (P("dp", None), P(("dp", "proto"), None))
    return jax.shard_map(shards, mesh=mesh, in_specs=in_specs, out_specs=out_specs, check_vma=False)
```

time: 997 us -> 110 us (0.11)
  waiting for transfers between devices: 786 us -> 0 us
  matrix products: 120 us -> 0 us
  Pallas kernels: 0 us -> 106 us
  blocking collectives: 31.7 us -> 0 us
  other arithmetic: 26.7 us -> 0 us
  between operations: 14.7 us -> 0.65 us
    psum x4 -> x0, waiting for transfers between devices: 507 us -> none  [the longest x3 475 us: shards(): col_total = lax.psum(col_local, 'dp')]
    reduce_scatter x1 -> x0, waiting for transfers between devices: 191 us -> none  [shards(): lax.psum_scatter(lax.dot_general(logit_grad, student_bf, (((0,), (0,)), (...]
    dot_general x10 -> x0, matrix products: 120 us -> none  [the longest x3 48.2 us: shards(): row_local = jnp.dot(teacher_exp, col_scale, precision=lax.Precision.HIGHEST)]
    pallas_call x0 -> x1, Pallas kernels: none -> 106 us  [shards(): pl.pallas_call(kernel, out_shape=[jax.ShapeDtypeStruct((B, B), f32), jax....]
    all_gather x1 -> x0, waiting for transfers between devices: 87.6 us -> none  [shards(): gathered = lax.all_gather(prototypes, 'dp', axis=0, tiled=True)]
    psum x3 -> x0, blocking collectives: 31.7 us -> none  [shards(): row_total = lax.psum(row_local, 'proto')]
    convert_element_type x1 -> x0, other arithmetic: 11.7 us -> none  [shards(): (loss_scale * (student_exp / partition[:, None] - targets) / student_temp...]
  transfers between devices with their start and end apart: 6 -> 0, of which waited for: 6 -> 0; matrix products, arithmetic and copies ran while one was open for 3% -> 0% of each run, Pallas kernels for 0% -> 0%
where the time goes in v1:
time: 110 us; the launch traced here: 109 us
  Pallas kernels  106 us (96%)
  local copies, waits for them, and re-layouts  2.42 us (2%)
    pallas_call x1, Pallas kernels, shards(): pl.pallas_call(kernel, out_shape=[jax.ShapeDtypeStruct((B, B), f32), jax....  106 us
    unnamed x4, local copies, waits for them, and re-layouts  2.42 us

profile of v1, /device:TPU:32, one launch (start us, length us, event | category | flops | bytes accessed | tf_op | source)
XLA Modules:
  0.0 108.9 jit_solution(12847104972784213498)
XLA Ops:
  0.6 105.8 %shard_map.50 = (f32[256,256]{1,0:T(8,128)}, f32[256,256]{1,0:T(8,128)}) custom-call(bf16[256,256]{1,0:T(8,128)(2,1)} %student_ref.1, bf16[256,256]{1,0:T(8,128)(2,1)} %teacher_ref.1, bf16[256,256]{1,0:T(8,128)(2,1)} %proto_ref.1), custom_call_target="tpu_custom_call" | custom-call | tf_op jit(solution)/shard_map/pallas_call | solution.py:452
  106.4 0.0 copy-start
  106.5 1.7 %copy.7 = f32[256,256]{1,0:T(8,128)} copy(f32[256,256]{1,0:T(8,128)} %get-tuple-element.4) | data formatting | bytes 524288
  108.2 0.0 copy-done
  108.2 0.7 copy.8
Async XLA Ops:
  106.4 1.7 %copy-start = (f32[256,256]{1,0:T(8,128)S(1)}, f32[256,256]{1,0:T(8,128)}, u32[]{:S(2)}) copy-start(f32[256,256]{1,0:T(8,128)} %get-tuple-element.5) | copy-start | bytes 786436

commit v2 on v1

v2 whole, which is shorter than its diff:
```python
import math

import jax
import jax.numpy as jnp
from jax import lax
from jax.experimental import pallas as pl
from jax.experimental.pallas import tpu as pltpu
from jax.sharding import PartitionSpec as P

NZ, NY, NX, NC = 8, 4, 4, 2
B = 256
ROWS = NY * NC * B
COLS = NZ * B
CROPS = 16384
PROTOS = 65536
SWEEPS = 3
teacher_temp = 0.07
student_temp = 0.1
loss_scale = 1024.0
epsilon = 1e-06
LOG2E = math.log2(math.e)
MESH = pl.DeviceIdType.MESH
NT = (((1,), (1,)), ((), ()))
f32 = jnp.float32
bf16 = jnp.bfloat16
SUB = 4
PIECE = B // SUB
H = B // 2
N_YX = NY * NX - 1
OFFSET = (0, 8, 24, 32)
AG, CROP, FORWARD, COL, SIB, ROW, RING, US, V, QS, GROUPS = 0, 1, 3, 5, 6, 7, 8, 9, 10, 11, 12


def unit_rows(matrix):
    values = matrix.astype(f32)
    inverse = lax.rsqrt(jnp.sum(values * values, axis=-1, keepdims=True) + epsilon)
    return values * inverse, inverse


def kernel(
    student_ref, teacher_ref, proto_ref, gs_ref, gp_ref,
    protos, teach, stud, stud_t, t_exp, s_exp, grad, part, row_a, row_b, mat,
    col_send, col_recv, row_sib, row_send, sib_recv, row_recv,
    chunk, ring_send, ring_recv, u_ref, u_send, u_sib, v_send, v_recv, q_full,
    ss, ag_rs, hop_rs, far_rs, fw_rs, col_rs, sib_rs, row_rs, rg_rs, us_rs, vq_rs,
):
    dp = lax.axis_index("dp")
    x = lax.axis_index("proto")
    z, y, c = dp // (NY * NC), (dp // NC) % NY, dp % NC

    def dev(dz, dy, flip, dx):
        core = 1 - c if flip else c
        return ((((z + dz) % NZ) * NY + (y + dy) % NY) * NC + core, (x + dx) % NX)

    right, left, sibling = dev(1, 0, 0, 0), dev(NZ - 1, 0, 0, 0), dev(0, 0, 1, 0)
    up, down = dev(0, 1, 0, 0), dev(0, NY - 1, 0, 0)
    z_peers = [(o, dev(o, 0, 0, 0)) for o in (4, 3, 5, 2, 6, 1, 7)]
    far = sorted(
        ((a, b) for a in range(NY) for b in range(NX) if (a, b) != (0, 0)),
        key=lambda ab: -min(ab[0], NY - ab[0]) - min(ab[1], NX - ab[1]),
    )
    yx_peers = [((a, b), dev(0, a, 0, b)) for a, b in far]

    def copy(src, dst, group, rs, to):
        return pltpu.make_async_remote_copy(
            src_ref=src, dst_ref=dst, send_sem=ss.at[group], recv_sem=rs, device_id=to, device_id_type=MESH
        )

    def wait_recv(ref, rs):
        copy(ref, ref, 0, rs, right).wait_recv()

    def wait_send(ref, group):
        copy(ref, ref, group, vq_rs.at[0], right).wait_send()

    barrier = pltpu.get_barrier_semaphore()
    near = [right, left, up, down, sibling] + [dev(0, 0, 0, b) for b in (2, 1, 3)]
    for peer in near:
        pl.semaphore_signal(barrier, inc=1, device_id=peer, device_id_type=MESH)

    protos[0:B, :] = unit_rows(proto_ref[...])[0].astype(bf16)
    teach[0:B, :] = unit_rows(teacher_ref[...])[0].astype(bf16)
    stud[0:B, :] = unit_rows(student_ref[...])[0].astype(bf16)
    pl.semaphore_wait(barrier, len(near))

    ag = {}

    def ag_step(k):
        for s in range(SUB):
            for d in (0, 1):
                if k == 3 and (2 * s) // SUB != d:
                    continue
                if k > 0:
                    ag[(k - 1, s, d)].wait_recv()
                src = (NZ - k) % NZ if d == 0 else k
                dst = NZ - k - 1 if d == 0 else k + 1
                cp = copy(
                    protos.at[pl.ds(src * B + s * PIECE, PIECE)],
                    protos.at[pl.ds(dst * B + s * PIECE, PIECE)],
                    AG, ag_rs.at[k, s, d], right if d == 0 else left,
                )
                cp.start()
                ag[(k, s, d)] = cp

    def ag_wait(k):
        for s in range(SUB):
            for d in (0, 1):
                cp = ag.get((k, s, d))
                if cp is not None:
                    cp.wait_recv()

    hop, last = {}, {}
    crops = (teach, stud)

    def forward(w, j):
        ref = crops[w]
        copy(
            ref.at[pl.ds(2 * j * B, B)], ref.at[pl.ds((2 * j + 1) * B, B)], FORWARD + w, fw_rs.at[w], sibling
        ).start()

    def crop_start(w):
        ref = crops[w]
        for first in (0, 1):
            for d, to, j in ((0, up, 3), (1, down, 1)):
                h = first if d == 0 else 1 - first
                cp = copy(
                    ref.at[pl.ds(h * H, H)], ref.at[pl.ds(2 * j * B + h * H, H)],
                    CROP + w, hop_rs.at[w, d, h], to,
                )
                cp.start()
                hop[(w, d, h)] = cp
        forward(w, 0)

    def crop_relay(w):
        ref = crops[w]
        for d, to, j in ((0, up, 3), (1, down, 1)):
            hop[(w, d, d)].wait_recv()
            cp = copy(
                ref.at[pl.ds(2 * j * B + d * H, H)], ref.at[pl.ds(4 * B + d * H, H)],
                CROP + w, far_rs.at[w, d], to,
            )
            cp.start()
            last[(w, d)] = cp
        for d, j in ((0, 3), (1, 1)):
            hop[(w, d, 1 - d)].wait_recv()
            forward(w, j)

    def crop_last(w):
        for d in (0, 1):
            last[(w, d)].wait_recv()
        forward(w, 2)

    def crop_wait(w):
        wait_recv(crops[w].at[pl.ds(0, NY * B)], fw_rs.at[w])

    lane_tiles = COLS // 128

    def teacher_slot(s):
        cols = slice(s * B, (s + 1) * B)
        dots = lax.dot_general(teach[...], protos[cols, :], NT, preferred_element_type=f32)
        values = jnp.exp2(dots * (LOG2E / teacher_temp))
        t_exp[:, cols] = values
        col_send[0, s:s + 1, :] = jnp.sum(values, axis=0, keepdims=True)

    def student_slot(s):
        cols = slice(s * B, (s + 1) * B)
        dots = lax.dot_general(stud[...], protos[cols, :], NT, preferred_element_type=f32)
        values = jnp.exp2(dots * (LOG2E / student_temp))
        s_exp[:, cols] = values
        both = values[:, :128] + values[:, 128:]
        part[...] = both if s == 0 else part[...] + both

    ag_step(0)
    crop_start(0)
    crop_start(1)
    ag_step(1)
    crop_relay(0)
    ag_step(2)
    crop_last(0)
    crop_relay(1)
    ag_step(3)
    crop_wait(0)
    for s in (0, 1, 7, 2, 6):
        teacher_slot(s)
    for s in range(SUB):
        ag[(2, s, 1 - (2 * s) // SUB)].wait_recv()
    teacher_slot(3)
    teacher_slot(5)
    ag_wait(3)
    teacher_slot(4)

    def start_col(n):
        for o, peer in z_peers:
            copy(col_send.at[n], col_recv.at[n, NZ - o - 1], COL, col_rs.at[n], peer).start()

    def finish_col(n):
        total = col_send[n]
        wait_recv(col_recv.at[n], col_rs.at[n])
        for o in range(1, NZ):
            total = total + pltpu.roll(col_recv[n, o - 1], o, 0)
        return 1.0 / (PROTOS * total)

    def start_sibling(n):
        at = pl.ds(OFFSET[n], OFFSET[n + 1] - OFFSET[n])
        copy(row_sib.at[at], sib_recv.at[at], SIB, sib_rs.at[n], sibling).start()

    even = lax.broadcasted_iota(jnp.int32, (8, B), 0) % 2 == 0

    def swap(v):
        return jnp.where(even, pltpu.roll(v, 7, 0), pltpu.roll(v, 1, 0))

    def start_row(n):
        start, height = OFFSET[n], OFFSET[n + 1] - OFFSET[n]
        at = pl.ds(start, height)
        wait_recv(sib_recv.at[at], sib_rs.at[n])
        for h in range(start, start + height, 8):
            row_send[h:h + 8, :] = row_sib[h:h + 8, :] + swap(sib_recv[h:h + 8, :])
        for (a, b), peer in yx_peers:
            t = ((NY - a) % NY) * NX + (NX - b) % NX - 1
            to = row_recv.at[pl.ds(N_YX * start + t * height, height)]
            copy(row_send.at[at], to, ROW, row_rs.at[n], peer).start()

    def finish_row(n):
        start, height = OFFSET[n], OFFSET[n + 1] - OFFSET[n]
        wait_recv(row_recv.at[pl.ds(N_YX * start, N_YX * height)], row_rs.at[n])
        out = []
        for h in range(0, height, 8):
            total = row_send[start + h:start + h + 8, :]
            for a in range(NY):
                some = None
                for b in range(NX):
                    if (a, b) == (0, 0):
                        continue
                    k = N_YX * start + (a * NX + b - 1) * height + h
                    v = row_recv[k:k + 8, :]
                    some = v if some is None else some + v
                total = total + (some if a == 0 else pltpu.roll(some, 2 * a, 0))
            out.append(total)
        return out

    lane = lax.broadcasted_iota(jnp.int32, (B, 128), 1)

    def to_lanes(at):
        row_sib[at:at + 8, :] = jnp.transpose(mat[...])[0:8, :]

    def to_rows(v, out):
        wide = jnp.transpose(jnp.concatenate([v, jnp.zeros((120, B), f32)], axis=0))
        for q in range(8):
            out[q * B:(q + 1) * B, :] = jnp.broadcast_to(wide[:, q:q + 1], (B, 128))

    def row_pass(col):
        mat[...] = jnp.zeros((B, 128), f32)

        def body(q, _):
            rows = pl.ds(pl.multiple_of(q * B, B), B)
            acc = jnp.zeros((B, 128), f32)
            for t in range(lane_tiles):
                s, h = t // 2, t % 2
                acc = acc + t_exp[rows, t * 128:(t + 1) * 128] * col[s:s + 1, h * 128:(h + 1) * 128]
            mat[...] = jnp.where(lane == q, jnp.sum(acc, axis=1, keepdims=True), mat[...])
            return 0

        lax.fori_loop(0, 8, body, 0)

    def partition_pass():
        mat[...] = jnp.zeros((B, 128), f32)

        def body(q, _):
            rows = pl.ds(pl.multiple_of(q * B, B), B)
            mat[...] = jnp.where(lane == q, jnp.sum(part[rows, :], axis=1, keepdims=True), mat[...])
            return 0

        lax.fori_loop(0, 8, body, 0)

    def col_pass(n):
        def body(i, acc):
            rows = pl.ds(pl.multiple_of(i * 64, 64), 64)
            scale = jnp.concatenate([row_b[rows, :]] * lane_tiles, axis=1)
            values = t_exp[rows, :] * scale
            return acc + jnp.sum(values.reshape(8, 8, COLS), axis=0)

        acc = lax.fori_loop(0, ROWS // 64, body, jnp.zeros((8, COLS), f32))
        total = jnp.sum(acc, axis=0, keepdims=True)
        for s in range(NZ):
            col_send[n, s:s + 1, :] = total[:, s * B:(s + 1) * B]

    start_col(0)
    crop_last(1)
    crop_wait(1)
    for s in range(4):
        student_slot(s)
    row_pass(finish_col(0))
    to_lanes(OFFSET[0])
    start_sibling(0)
    start_row(0)
    for s in range(4, 8):
        student_slot(s)
    (row_total,) = finish_row(0)
    to_rows(1.0 / (CROPS * row_total), row_b)
    col_pass(1)
    start_col(1)
    partition_pass()
    to_lanes(OFFSET[1] + 8)
    for q in range(8):
        stud_t[:, q * B:(q + 1) * B] = jnp.transpose(stud[q * B:(q + 1) * B, :].astype(f32)).astype(bf16)
    row_pass(finish_col(1))
    to_lanes(OFFSET[1])
    start_sibling(1)
    start_row(1)
    row_total, partition = finish_row(1)
    to_rows(1.0 / (CROPS * row_total), row_b)
    col_pass(2)
    start_col(2)
    to_rows((loss_scale / student_temp) / partition, row_a)
    col = finish_col(2)
    row_pass(col)
    to_lanes(OFFSET[2])
    start_sibling(2)
    start_row(2)
    (row_total,) = finish_row(2)
    to_rows((loss_scale / student_temp) / row_total, row_b)

    def grad_part(start, height, slots):
        for r in range(start, start + height, 16):
            rows = slice(r, r + 16)
            a = row_a[rows, :]
            b = row_b[rows, :]
            for s in slots:
                for h in range(2):
                    at = slice(s * B + h * 128, s * B + (h + 1) * 128)
                    scale = col[s:s + 1, h * 128:(h + 1) * 128]
                    grad[rows, at] = (s_exp[rows, at] * a - t_exp[rows, at] * b * scale).astype(bf16)

    def chunk_dot(s):
        chunk[s] = jnp.dot(stud_t[...], grad[:, s * B:(s + 1) * B], preferred_element_type=f32)

    rg = {}

    def ring(m, d, pieces):
        s = 4 - m if d == 0 else 4 + m
        for p in pieces:
            rows = slice(p * PIECE, (p + 1) * PIECE)
            value = chunk[s, rows, :]
            if (m - 1, d, p) in rg:
                rg[(m - 1, d, p)].wait_recv()
                value = value + ring_recv[2 * (m - 1) + d, rows, :].astype(f32)
            ring_send[2 * m + d, rows, :] = value.astype(bf16)
            at = pl.ds(p * PIECE, PIECE)
            cp = copy(
                ring_send.at[2 * m + d, at], ring_recv.at[2 * m + d, at],
                RING, rg_rs.at[m, d, p], right if d == 0 else left,
            )
            cp.start()
            rg[(m, d, p)] = cp

    low, high = range(SUB // 2), range(SUB // 2, SUB)

    def u_dot(q):
        return jnp.dot(grad[q * B:(q + 1) * B, :], protos[...], preferred_element_type=f32)

    us = {}

    def u_pair(j, slots):
        grad_part((2 * j + 1) * B, B, slots)
        grad_part(2 * j * B, B, slots)
        u_send[j] = u_dot(2 * j + 1).astype(bf16)
        cp = copy(u_send.at[j], u_sib.at[j], US, us_rs.at[j], sibling)
        cp.start()
        us[j] = cp
        u_ref[j] = u_dot(2 * j)

    Q = B // NX
    mine = pl.ds(pl.multiple_of(x * Q, Q), Q)

    def v_start(j):
        us[j].wait_recv()
        total = u_ref[j] + u_sib[j].astype(f32)
        if j == 0:
            u_ref[j] = total
        v_send[j] = total.astype(bf16)
        for b in (2, 1, 3, 0):
            if (j, b) == (0, 0):
                continue
            t = ((NY - j) % NY) * NX + (NX - b) % NX - 1
            at = pl.multiple_of(((x + b) % NX) * Q, Q)
            copy(v_send.at[j, pl.ds(at, Q)], v_recv.at[t], V, vq_rs.at[0], dev(0, j, 0, b)).start()

    grad_part(0, ROWS, (4,))
    chunk_dot(4)
    ring(0, 0, low)
    ring(0, 1, high)
    grad_part(0, ROWS, (3, 5))
    chunk_dot(3)
    ring(1, 0, high)
    chunk_dot(5)
    ring(1, 1, low)
    rest = (0, 1, 2, 6, 7)
    u_pair(2, rest)
    u_pair(1, rest)
    ring(1, 0, low)
    ring(1, 1, high)
    v_start(2)
    u_pair(3, rest)
    v_start(1)
    u_pair(0, rest)
    v_start(3)
    chunk_dot(2)
    ring(2, 0, high)
    chunk_dot(6)
    ring(2, 1, low)
    v_start(0)
    ring(2, 0, low)
    ring(2, 1, high)
    chunk_dot(1)
    ring(3, 0, high)
    chunk_dot(7)
    ring(3, 1, low)
    chunk_dot(0)
    ring(3, 0, low)
    ring(3, 1, high)

    wait_recv(v_recv, vq_rs.at[0])
    total = u_ref[0, mine, :]
    for i in range(N_YX):
        total = total + v_recv[i].astype(f32)
    unit, inverse = unit_rows(student_ref[mine, :])
    q_full[mine, :] = (inverse * (total - unit * jnp.sum(unit * total, axis=1, keepdims=True))).astype(bf16)
    for b in (2, 1, 3):
        copy(q_full.at[mine], q_full.at[mine], QS, vq_rs.at[1], dev(0, 0, 0, b)).start()

    for m, d, p in rg:
        if m == 3:
            rg[(m, d, p)].wait_recv()
    total = chunk[0] + ring_recv[6].astype(f32) + ring_recv[7].astype(f32)
    total = jnp.transpose(total)
    unit, inverse = unit_rows(proto_ref[...])
    gp_ref[...] = inverse * (total - unit * jnp.sum(unit * total, axis=1, keepdims=True))

    wait_recv(q_full.at[pl.ds(0, (NX - 1) * Q)], vq_rs.at[1])
    gs_ref[...] = q_full[...].astype(f32)

    wait_send(protos.at[pl.ds(0, 7 * B)], AG)
    for w in (0, 1):
        wait_send(crops[w].at[pl.ds(0, 3 * B)], CROP + w)
        wait_send(crops[w].at[pl.ds(0, 4 * B)], FORWARD + w)
    wait_send(col_recv, COL)
    wait_send(row_sib, SIB)
    wait_send(row_recv, ROW)
    wait_send(ring_recv.at[pl.ds(0, 7)], RING)
    wait_send(u_sib, US)
    wait_send(v_recv, V)
    wait_send(q_full.at[pl.ds(0, (NX - 1) * Q)], QS)


def shards(student_feat, teacher_feat, prototypes):
    vmem = pltpu.VMEM
    dma = pltpu.SemaphoreType.DMA
    sems = [
        dma((GROUPS,)), dma((4, SUB, 2)), dma((2, 2, 2)), dma((2, 2)), dma((2,)), dma((SWEEPS,)), dma((SWEEPS,)),
        dma((SWEEPS,)), dma((4, 2, SUB)), dma((NY,)), dma((2,)),
    ]
    return pl.pallas_call(
        kernel,
        out_shape=[jax.ShapeDtypeStruct((B, B), f32), jax.ShapeDtypeStruct((B, B), f32)],
        in_specs=[pl.BlockSpec(memory_space=pltpu.VMEM)] * 3,
        out_specs=[pl.BlockSpec(memory_space=pltpu.VMEM)] * 2,
        scratch_shapes=[
            vmem((COLS, B), bf16),
            vmem((ROWS, B), bf16),
            vmem((ROWS, B), bf16),
            vmem((B, ROWS), bf16),
            vmem((ROWS, COLS), f32),
            vmem((ROWS, COLS), f32),
            vmem((ROWS, COLS), bf16),
            vmem((ROWS, 128), f32),
            vmem((ROWS, 128), f32),
            vmem((ROWS, 128), f32),
            vmem((B, 128), f32),
            vmem((SWEEPS, 8, B), f32),
            vmem((SWEEPS, NZ - 1, 8, B), f32),
            vmem((OFFSET[-1], B), f32),
            vmem((OFFSET[-1], B), f32),
            vmem((OFFSET[-1], B), f32),
            vmem((N_YX * OFFSET[-1], B), f32),
            vmem((NZ, B, B), f32),
            vmem((8, B, B), bf16),
            vmem((8, B, B), bf16),
            vmem((NY, B, B), f32),
            vmem((NY, B, B), bf16),
            vmem((NY, B, B), bf16),
            vmem((NY, B, B), bf16),
            vmem((N_YX, B // NX, B), bf16),
            vmem((B, B), bf16),
        ] + sems,
        compiler_params=pltpu.CompilerParams(
            collective_id=0, has_side_effects=True, vmem_limit_bytes=63 * 2**20
        ),
    )(student_feat, teacher_feat, prototypes)


def solution(mesh):
    in_specs = (P("dp", None), P("dp", None), P(("dp", "proto"), None))
    out_specs = (P("dp", None), P(("dp", "proto"), None))
    return jax.shard_map(shards, mesh=mesh, in_specs=in_specs, out_specs=out_specs, check_vma=False)
```

time: 110 us -> 90.8 us (0.83)
  Pallas kernels: 106 us -> 87 us
    pallas_call x1, Pallas kernels: 106 us -> 87 us  [shards(): pl.pallas_call(kernel, out_shape=[jax.ShapeDtypeStruct((B, B), f32), jax....]
where the time goes in v2:
time: 90.8 us; the launch traced here: 90 us
  Pallas kernels  87 us (96%)
  local copies, waits for them, and re-layouts  2.42 us (3%)
    pallas_call x1, Pallas kernels, shards(): pl.pallas_call(kernel, out_shape=[jax.ShapeDtypeStruct((B, B), f32), jax....  87 us
    unnamed x4, local copies, waits for them, and re-layouts  2.42 us

profile of v2, /device:TPU:32, one launch (start us, length us, event | category | flops | bytes accessed | tf_op | source)
XLA Modules:
  0.0 90.0 jit_solution(5157440804793050086)
XLA Ops:
  0.6 87.0 %shard_map.50 = (f32[256,256]{1,0:T(8,128)}, f32[256,256]{1,0:T(8,128)}) custom-call(bf16[256,256]{1,0:T(8,128)(2,1)} %student_ref.1, bf16[256,256]{1,0:T(8,128)(2,1)} %teacher_ref.1, bf16[256,256]{1,0:T(8,128)(2,1)} %proto_ref.1), custom_call_target="tpu_custom_call" | custom-call | tf_op jit(solution)/shard_map/pallas_call | solution.py:461
  87.6 0.0 copy-start
  87.6 1.7 %copy.7 = f32[256,256]{1,0:T(8,128)} copy(f32[256,256]{1,0:T(8,128)} %get-tuple-element.4) | data formatting | bytes 524288
  89.3 0.0 copy-done
  89.3 0.7 copy.8
Async XLA Ops:
  87.6 1.7 %copy-start = (f32[256,256]{1,0:T(8,128)S(1)}, f32[256,256]{1,0:T(8,128)}, u32[]{:S(2)}) copy-start(f32[256,256]{1,0:T(8,128)} %get-tuple-element.5) | copy-start | bytes 786436

commit v3 on v2

v3 whole, which is shorter than its diff:
```python
import math

import jax
import jax.numpy as jnp
from jax import lax
from jax.experimental import pallas as pl
from jax.experimental.pallas import tpu as pltpu
from jax.sharding import PartitionSpec as P

NZ, NY, NX, NC = 8, 4, 4, 2
B = 256
ROWS = NY * NC * B
COLS = NZ * B
CROPS = 16384
PROTOS = 65536
SWEEPS = 3
teacher_temp = 0.07
student_temp = 0.1
loss_scale = 1024.0
epsilon = 1e-06
LOG2E = math.log2(math.e)
MESH = pl.DeviceIdType.MESH
NT = (((1,), (1,)), ((), ()))
f32 = jnp.float32
bf16 = jnp.bfloat16
SUB = 4
PIECE = B // SUB
H = B // 2
N_YX = NY * NX - 1
OFFSET = (0, 8, 24, 32)
AG, CROP, FORWARD, COL, SIB, ROW, RING, US, V, QS, GROUPS = 0, 1, 3, 5, 6, 7, 8, 9, 10, 11, 12


def unit_rows(matrix):
    values = matrix.astype(f32)
    inverse = lax.rsqrt(jnp.sum(values * values, axis=-1, keepdims=True) + epsilon)
    return values * inverse, inverse


def kernel(
    student_ref, teacher_ref, proto_ref, gs_ref, gp_ref,
    protos, teach, stud, stud_t, t_exp, s_exp, grad, part, row_a, row_b, mat,
    col_send, col_recv, row_sib, row_send, sib_recv, row_recv,
    chunk, ring_send, ring_recv, u_ref, u_send, u_sib, v_send, v_recv, q_full,
    ss, ag_rs, far_ag_rs, hop_rs, far_rs, fw_rs, col_rs, sib_rs, row_rs, rg_rs, us_rs, vq_rs,
):
    dp = lax.axis_index("dp")
    x = lax.axis_index("proto")
    z, y, c = dp // (NY * NC), (dp // NC) % NY, dp % NC

    def dev(dz, dy, flip, dx):
        core = 1 - c if flip else c
        return ((((z + dz) % NZ) * NY + (y + dy) % NY) * NC + core, (x + dx) % NX)

    right, left, sibling = dev(1, 0, 0, 0), dev(NZ - 1, 0, 0, 0), dev(0, 0, 1, 0)
    right2, left2 = dev(2, 0, 0, 0), dev(NZ - 2, 0, 0, 0)
    up, down = dev(0, 1, 0, 0), dev(0, NY - 1, 0, 0)
    z_peers = [(o, dev(o, 0, 0, 0)) for o in (4, 3, 5, 2, 6, 1, 7)]
    far = sorted(
        ((a, b) for a in range(NY) for b in range(NX) if (a, b) != (0, 0)),
        key=lambda ab: -min(ab[0], NY - ab[0]) - min(ab[1], NX - ab[1]),
    )
    yx_peers = [((a, b), dev(0, a, 0, b)) for a, b in far]

    def copy(src, dst, group, rs, to):
        return pltpu.make_async_remote_copy(
            src_ref=src, dst_ref=dst, send_sem=ss.at[group], recv_sem=rs, device_id=to, device_id_type=MESH
        )

    def wait_recv(ref, rs):
        copy(ref, ref, 0, rs, right).wait_recv()

    def wait_send(ref, group):
        copy(ref, ref, group, vq_rs.at[0], right).wait_send()

    barrier = pltpu.get_barrier_semaphore()
    near = [right2, left2, right, left, up, down, sibling] + [dev(0, 0, 0, b) for b in (2, 1, 3)]
    for peer in near:
        pl.semaphore_signal(barrier, inc=1, device_id=peer, device_id_type=MESH)

    protos[0:B, :] = unit_rows(proto_ref[...])[0].astype(bf16)
    teach[0:B, :] = unit_rows(teacher_ref[...])[0].astype(bf16)
    stud[0:B, :] = unit_rows(student_ref[...])[0].astype(bf16)
    pl.semaphore_wait(barrier, len(near))

    low, high = tuple(range(SUB // 2)), tuple(range(SUB // 2, SUB))
    every = low + high
    ways = ((0, right, right2, low, high), (1, left, left2, high, low))

    def block(k, d, p):
        slot = (NZ - k) % NZ if d == 0 else k
        return protos.at[pl.ds(slot * B + p * PIECE, PIECE)]

    def ag_step(k):
        for i in range(SUB):
            for d, to1, to2, first, then in ways:
                p = (first + then)[i]
                if k > 0:
                    wait_recv(block(k, d, p), ag_rs.at[k - 1, d, p])
                if k == 2 and p in first:
                    copy(block(2, d, p), block(4, d, p), AG, far_ag_rs.at[d], to2).start()
                copy(block(k, d, p), block(k + 1, d, p), AG, ag_rs.at[k, d, p], to1).start()

    def ag_wait():
        for d in (0, 1):
            for p in every:
                wait_recv(block(3, d, p), ag_rs.at[2, d, p])

    def ag_wait_far():
        for d in (0, 1):
            wait_recv(protos.at[pl.ds(0, H)], far_ag_rs.at[d])

    hop, last = {}, {}
    crops = (teach, stud)

    def forward(w, j):
        ref = crops[w]
        copy(
            ref.at[pl.ds(2 * j * B, B)], ref.at[pl.ds((2 * j + 1) * B, B)], FORWARD + w, fw_rs.at[w], sibling
        ).start()

    def crop_start(w):
        ref = crops[w]
        for first in (0, 1):
            for d, to, j in ((0, up, 3), (1, down, 1)):
                h = first if d == 0 else 1 - first
                cp = copy(
                    ref.at[pl.ds(h * H, H)], ref.at[pl.ds(2 * j * B + h * H, H)],
                    CROP + w, hop_rs.at[w, d, h], to,
                )
                cp.start()
                hop[(w, d, h)] = cp
        forward(w, 0)

    def crop_relay(w):
        ref = crops[w]
        for d, to, j in ((0, up, 3), (1, down, 1)):
            hop[(w, d, d)].wait_recv()
            cp = copy(
                ref.at[pl.ds(2 * j * B + d * H, H)], ref.at[pl.ds(4 * B + d * H, H)],
                CROP + w, far_rs.at[w, d], to,
            )
            cp.start()
            last[(w, d)] = cp
        for d, j in ((0, 3), (1, 1)):
            hop[(w, d, 1 - d)].wait_recv()
            forward(w, j)

    def crop_last(w):
        for d in (0, 1):
            last[(w, d)].wait_recv()
        forward(w, 2)

    def crop_wait(w):
        wait_recv(crops[w].at[pl.ds(0, NY * B)], fw_rs.at[w])

    def teacher_slot(s):
        cols = slice(s * B, (s + 1) * B)
        dots = lax.dot_general(teach[...], protos[cols, :], NT, preferred_element_type=f32)
        values = jnp.exp2(dots * (LOG2E / teacher_temp))
        t_exp[:, cols] = values
        total = jnp.sum(values, axis=0, keepdims=True)
        for h in (0, 1):
            col_send[0, h, s:s + 1, :] = total[:, h * 128:(h + 1) * 128]

    def student_slot(s):
        cols = slice(s * B, (s + 1) * B)
        dots = lax.dot_general(stud[...], protos[cols, :], NT, preferred_element_type=f32)
        values = jnp.exp2(dots * (LOG2E / student_temp))
        s_exp[:, cols] = values
        both = values[:, :128] + values[:, 128:]
        part[...] = both if s == 0 else part[...] + both

    ag_step(0)
    crop_start(0)
    crop_start(1)
    ag_step(1)
    crop_relay(0)
    ag_step(2)
    crop_last(0)
    crop_wait(0)
    for s in (0, 1, 7, 2, 6):
        teacher_slot(s)
    crop_relay(1)
    ag_wait()
    teacher_slot(3)
    teacher_slot(5)
    ag_wait_far()
    teacher_slot(4)

    def tile(s, h):
        return slice(s * B + h * 128, s * B + (h + 1) * 128)

    def start_col(n, h):
        for o, peer in z_peers:
            copy(col_send.at[n, h], col_recv.at[n, h, NZ - o - 1], COL, col_rs.at[n, h], peer).start()

    def finish_col(n, h):
        total = col_send[n, h]
        wait_recv(col_recv.at[n, h], col_rs.at[n, h])
        for o in range(1, NZ):
            total = total + pltpu.roll(col_recv[n, h, o - 1], o, 0)
        return 1.0 / (PROTOS * total)

    def start_sibling(n, g):
        at = pl.ds(OFFSET[n], OFFSET[n + 1] - OFFSET[n])
        copy(row_sib.at[g, at], sib_recv.at[g, at], SIB, sib_rs.at[n, g], sibling).start()

    even = lax.broadcasted_iota(jnp.int32, (8, 128), 0) % 2 == 0

    def swap(v):
        return jnp.where(even, pltpu.roll(v, 7, 0), pltpu.roll(v, 1, 0))

    def start_row(n, g):
        start, height = OFFSET[n], OFFSET[n + 1] - OFFSET[n]
        at = pl.ds(start, height)
        wait_recv(sib_recv.at[g, at], sib_rs.at[n, g])
        for i in range(start, start + height, 8):
            row_send[g, i:i + 8, :] = row_sib[g, i:i + 8, :] + swap(sib_recv[g, i:i + 8, :])
        for (a, b), peer in yx_peers:
            t = ((NY - a) % NY) * NX + (NX - b) % NX - 1
            to = row_recv.at[g, pl.ds(N_YX * start + t * height, height)]
            copy(row_send.at[g, at], to, ROW, row_rs.at[n, g], peer).start()

    def finish_row(n, g):
        start, height = OFFSET[n], OFFSET[n + 1] - OFFSET[n]
        wait_recv(row_recv.at[g, pl.ds(N_YX * start, N_YX * height)], row_rs.at[n, g])
        out = []
        for i in range(0, height, 8):
            total = row_send[g, start + i:start + i + 8, :]
            for a in range(NY):
                some = None
                for b in range(NX):
                    if (a, b) == (0, 0):
                        continue
                    k = N_YX * start + (a * NX + b - 1) * height + i
                    v = row_recv[g, k:k + 8, :]
                    some = v if some is None else some + v
                total = total + (some if a == 0 else pltpu.roll(some, 2 * a, 0))
            out.append(total)
        return out

    lane = lax.broadcasted_iota(jnp.int32, (128, 128), 1)

    def half_rows(q, g):
        return pl.ds(pl.multiple_of(q * B + g * 128, 128), 128)

    def to_lanes(g, at):
        row_sib[g, at:at + 8, :] = jnp.transpose(mat[...])[0:8, :]

    def to_rows(v, g, out):
        wide = jnp.transpose(jnp.concatenate([v, jnp.zeros((120, 128), f32)], axis=0))
        for q in range(8):
            out[q * B + g * 128:q * B + (g + 1) * 128, :] = jnp.broadcast_to(wide[:, q:q + 1], (128, 128))

    def row_first(col, acc):
        def body(q, _):
            rows = pl.ds(pl.multiple_of(q * B, B), B)
            total = t_exp[rows, tile(0, 0)] * col[0:1, :]
            for s in range(1, NZ):
                total = total + t_exp[rows, tile(s, 0)] * col[s:s + 1, :]
            acc[rows, :] = total
            return 0

        lax.fori_loop(0, 8, body, 0)

    def row_last(col, acc, g):
        mat[...] = jnp.zeros((128, 128), f32)

        def body(q, _):
            rows = half_rows(q, g)
            total = acc[rows, :]
            for s in range(NZ):
                total = total + t_exp[rows, tile(s, 1)] * col[s:s + 1, :]
            mat[...] = jnp.where(lane == q, jnp.sum(total, axis=1, keepdims=True), mat[...])
            return 0

        lax.fori_loop(0, 8, body, 0)

    def partition_sum(g):
        mat[...] = jnp.zeros((128, 128), f32)

        def body(q, _):
            total = jnp.sum(part[half_rows(q, g), :], axis=1, keepdims=True)
            mat[...] = jnp.where(lane == q, total, mat[...])
            return 0

        lax.fori_loop(0, 8, body, 0)

    def col_part(g, start, tiles):
        def body(q, acc):
            rows = half_rows(q, g)
            scale = row_b[rows, :]
            return tuple(
                v + jnp.sum((t_exp[rows, at] * scale).reshape(16, 8, 128), axis=0) for v, at in zip(acc, tiles)
            )

        return lax.fori_loop(0, 8, body, start)

    def row_to_col(n):
        zeros = jnp.zeros((8, 128), f32)
        both = [tile(s, h) for h in (0, 1) for s in range(NZ)]
        first = finish_row(n, 0)
        to_rows(1.0 / (CROPS * first[0]), 0, row_b)
        acc = col_part(0, (zeros,) * 16, both)
        second = finish_row(n, 1)
        to_rows(1.0 / (CROPS * second[0]), 1, row_b)
        for h in (0, 1):
            for s, v in enumerate(col_part(1, acc[h * 8:h * 8 + 8], both[h * 8:h * 8 + 8])):
                col_send[n + 1, h, s:s + 1, :] = jnp.sum(v, axis=0, keepdims=True)
            start_col(n + 1, h)
        return first[1:] + second[1:]

    def col_to_row(n, acc):
        first = finish_col(n, 0)
        row_first(first, acc)
        second = finish_col(n, 1)
        for g in (0, 1):
            row_last(second, acc, g)
            to_lanes(g, OFFSET[n])
            start_sibling(n, g)
        for g in (0, 1):
            start_row(n, g)
        return first, second

    start_col(0, 0)
    start_col(0, 1)
    crop_last(1)
    crop_wait(1)
    for s in range(4):
        student_slot(s)
    col_to_row(0, row_a)
    for s in range(4, 8):
        student_slot(s)
    row_to_col(0)
    for g in (0, 1):
        partition_sum(g)
        to_lanes(g, OFFSET[1] + 8)
    for q in range(8):
        stud_t[:, q * B:(q + 1) * B] = jnp.transpose(stud[q * B:(q + 1) * B, :].astype(f32)).astype(bf16)
    col_to_row(1, row_a)
    partition = row_to_col(1)
    for g in (0, 1):
        to_rows((loss_scale / student_temp) / partition[g], g, row_a)

    def scale_student(i, _):
        rows = pl.ds(pl.multiple_of(i * 64, 64), 64)
        scale = row_a[rows, :]
        for s in range(NZ):
            for h in (0, 1):
                s_exp[rows, tile(s, h)] = s_exp[rows, tile(s, h)] * scale
        return 0

    lax.fori_loop(0, ROWS // 64, scale_student, 0)
    col = col_to_row(2, part)

    def scale_teacher(i, _):
        rows = pl.ds(pl.multiple_of(i * 64, 64), 64)
        for s in range(NZ):
            for h in (0, 1):
                t_exp[rows, tile(s, h)] = t_exp[rows, tile(s, h)] * col[h][s:s + 1, :]
        return 0

    lax.fori_loop(0, ROWS // 64, scale_teacher, 0)
    for g in (0, 1):
        (row_total,) = finish_row(2, g)
        to_rows((loss_scale / student_temp) / row_total, g, row_b)

    def grad_part(start, height, slots):
        for r in range(start, start + height, 16):
            rows = slice(r, r + 16)
            scale = row_b[rows, :]
            for s in slots:
                for h in (0, 1):
                    at = tile(s, h)
                    grad[rows, at] = (s_exp[rows, at] - t_exp[rows, at] * scale).astype(bf16)

    def chunk_dot(s):
        chunk[s] = jnp.dot(stud_t[...], grad[:, s * B:(s + 1) * B], preferred_element_type=f32)

    def ring(m, d):
        s = 4 - m if d == 0 else 4 + m
        _, to1, to2, first, then = ways[d]
        for p in first if m == 0 else first + then:
            rows = slice(p * PIECE, (p + 1) * PIECE)
            at = pl.ds(p * PIECE, PIECE)
            value = chunk[s, rows, :]
            if m >= 2:
                wait_recv(ring_recv.at[2 * (m - 1) + d, at], rg_rs.at[m - 1, d, p])
                value = value + ring_recv[2 * (m - 1) + d, rows, :].astype(f32)
            if m == 2 and p in first:
                wait_recv(ring_recv.at[d, at], rg_rs.at[0, d, p])
                value = value + ring_recv[d, rows, :].astype(f32)
            ring_send[2 * m + d, rows, :] = value.astype(bf16)
            copy(
                ring_send.at[2 * m + d, at], ring_recv.at[2 * m + d, at], RING, rg_rs.at[m, d, p],
                to2 if m == 0 else to1,
            ).start()

    def u_dot(q):
        return jnp.dot(grad[q * B:(q + 1) * B, :], protos[...], preferred_element_type=f32)

    us = {}

    def u_pair(j, slots):
        grad_part((2 * j + 1) * B, B, slots)
        grad_part(2 * j * B, B, slots)
        u_send[j] = u_dot(2 * j + 1).astype(bf16)
        cp = copy(u_send.at[j], u_sib.at[j], US, us_rs.at[j], sibling)
        cp.start()
        us[j] = cp
        u_ref[j] = u_dot(2 * j)

    Q = B // NX
    mine = pl.ds(pl.multiple_of(x * Q, Q), Q)

    def v_start(j):
        us[j].wait_recv()
        total = u_ref[j] + u_sib[j].astype(f32)
        if j == 0:
            u_ref[j] = total
        v_send[j] = total.astype(bf16)
        for b in (2, 1, 3, 0):
            if (j, b) == (0, 0):
                continue
            t = ((NY - j) % NY) * NX + (NX - b) % NX - 1
            at = pl.multiple_of(((x + b) % NX) * Q, Q)
            copy(v_send.at[j, pl.ds(at, Q)], v_recv.at[t], V, vq_rs.at[0], dev(0, j, 0, b)).start()

    grad_part(0, ROWS, (3,))
    chunk_dot(3)
    ring(1, 0)
    grad_part(0, ROWS, (5,))
    chunk_dot(5)
    ring(1, 1)
    grad_part(0, ROWS, (4,))
    chunk_dot(4)
    ring(0, 0)
    ring(0, 1)
    rest = (0, 1, 2, 6, 7)
    u_pair(2, rest)
    u_pair(1, rest)
    v_start(2)
    u_pair(3, rest)
    v_start(1)
    u_pair(0, rest)
    chunk_dot(2)
    chunk_dot(6)
    ring(2, 0)
    ring(2, 1)
    v_start(3)
    v_start(0)
    chunk_dot(1)
    chunk_dot(7)
    chunk_dot(0)
    ring(3, 0)
    ring(3, 1)

    wait_recv(v_recv, vq_rs.at[0])
    total = u_ref[0, mine, :]
    for i in range(N_YX):
        total = total + v_recv[i].astype(f32)
    unit, inverse = unit_rows(student_ref[mine, :])
    q_full[mine, :] = (inverse * (total - unit * jnp.sum(unit * total, axis=1, keepdims=True))).astype(bf16)
    for b in (2, 1, 3):
        copy(q_full.at[mine], q_full.at[mine], QS, vq_rs.at[1], dev(0, 0, 0, b)).start()

    total = chunk[0]
    for d in (0, 1):
        for p in every:
            wait_recv(ring_recv.at[6 + d, pl.ds(p * PIECE, PIECE)], rg_rs.at[3, d, p])
        total = total + ring_recv[6 + d].astype(f32)
    total = jnp.transpose(total)
    unit, inverse = unit_rows(proto_ref[...])
    gp_ref[...] = inverse * (total - unit * jnp.sum(unit * total, axis=1, keepdims=True))

    wait_recv(q_full.at[pl.ds(0, (NX - 1) * Q)], vq_rs.at[1])
    gs_ref[...] = q_full[...].astype(f32)

    wait_send(protos.at[pl.ds(0, 7 * B)], AG)
    for w in (0, 1):
        wait_send(crops[w].at[pl.ds(0, 3 * B)], CROP + w)
        wait_send(crops[w].at[pl.ds(0, 4 * B)], FORWARD + w)
    wait_send(col_recv, COL)
    wait_send(row_sib, SIB)
    wait_send(row_recv, ROW)
    wait_send(ring_recv.at[pl.ds(0, 7)], RING)
    wait_send(u_sib, US)
    wait_send(v_recv, V)
    wait_send(q_full.at[pl.ds(0, (NX - 1) * Q)], QS)


def shards(student_feat, teacher_feat, prototypes):
    vmem = pltpu.VMEM
    dma = pltpu.SemaphoreType.DMA
    sems = [
        dma((GROUPS,)), dma((3, 2, SUB)), dma((2,)), dma((2, 2, 2)), dma((2, 2)), dma((2,)), dma((SWEEPS, 2)), dma((SWEEPS, 2)),
        dma((SWEEPS, 2)), dma((4, 2, SUB)), dma((NY,)), dma((2,)),
    ]
    return pl.pallas_call(
        kernel,
        out_shape=[jax.ShapeDtypeStruct((B, B), f32), jax.ShapeDtypeStruct((B, B), f32)],
        in_specs=[pl.BlockSpec(memory_space=pltpu.VMEM)] * 3,
        out_specs=[pl.BlockSpec(memory_space=pltpu.VMEM)] * 2,
        scratch_shapes=[
            vmem((COLS, B), bf16),
            vmem((ROWS, B), bf16),
            vmem((ROWS, B), bf16),
            vmem((B, ROWS), bf16),
            vmem((ROWS, COLS), f32),
            vmem((ROWS, COLS), f32),
            vmem((ROWS, COLS), bf16),
            vmem((ROWS, 128), f32),
            vmem((ROWS, 128), f32),
            vmem((ROWS, 128), f32),
            vmem((128, 128), f32),
            vmem((SWEEPS, 2, 8, 128), f32),
            vmem((SWEEPS, 2, NZ - 1, 8, 128), f32),
            vmem((2, OFFSET[-1], 128), f32),
            vmem((2, OFFSET[-1], 128), f32),
            vmem((2, OFFSET[-1], 128), f32),
            vmem((2, N_YX * OFFSET[-1], 128), f32),
            vmem((NZ, B, B), f32),
            vmem((8, B, B), bf16),
            vmem((8, B, B), bf16),
            vmem((NY, B, B), f32),
            vmem((NY, B, B), bf16),
            vmem((NY, B, B), bf16),
            vmem((NY, B, B), bf16),
            vmem((N_YX, B // NX, B), bf16),
            vmem((B, B), bf16),
        ] + sems,
        compiler_params=pltpu.CompilerParams(
            collective_id=0, has_side_effects=True, vmem_limit_bytes=63 * 2**20
        ),
    )(student_feat, teacher_feat, prototypes)


def solution(mesh):
    in_specs = (P("dp", None), P("dp", None), P(("dp", "proto"), None))
    out_specs = (P("dp", None), P(("dp", "proto"), None))
    return jax.shard_map(shards, mesh=mesh, in_specs=in_specs, out_specs=out_specs, check_vma=False)
```

time: 90.8 us -> 88.6 us (0.976)
  Pallas kernels: 87 us -> 85.4 us
    pallas_call x1, Pallas kernels: 87 us -> 85.4 us  [shards(): pl.pallas_call(kernel, out_shape=[jax.ShapeDtypeStruct((B, B), f32), jax....]
where the time goes in v3:
time: 88.6 us; the launch traced here: 88.5 us
  Pallas kernels  85.4 us (96%)
  local copies, waits for them, and re-layouts  2.42 us (3%)
    pallas_call x1, Pallas kernels, shards(): pl.pallas_call(kernel, out_shape=[jax.ShapeDtypeStruct((B, B), f32), jax....  85.4 us
    unnamed x4, local copies, waits for them, and re-layouts  2.42 us

profile of v3, /device:TPU:32, one launch (start us, length us, event | category | flops | bytes accessed | tf_op | source)
XLA Modules:
  0.0 88.5 jit_solution(4034924671441726055)
XLA Ops:
  0.6 85.4 %shard_map.50 = (f32[256,256]{1,0:T(8,128)}, f32[256,256]{1,0:T(8,128)}) custom-call(bf16[256,256]{1,0:T(8,128)(2,1)} %student_ref.1, bf16[256,256]{1,0:T(8,128)(2,1)} %teacher_ref.1, bf16[256,256]{1,0:T(8,128)(2,1)} %proto_ref.1), custom_call_target="tpu_custom_call" | custom-call | tf_op jit(solution)/shard_map/pallas_call | solution.py:500
  86.1 0.0 copy-start
  86.1 1.7 %copy.7 = f32[256,256]{1,0:T(8,128)} copy(f32[256,256]{1,0:T(8,128)} %get-tuple-element.4) | data formatting | bytes 524288
  87.8 0.0 copy-done
  87.8 0.7 copy.8
Async XLA Ops:
  86.1 1.7 %copy-start = (f32[256,256]{1,0:T(8,128)S(1)}, f32[256,256]{1,0:T(8,128)}, u32[]{:S(2)}) copy-start(f32[256,256]{1,0:T(8,128)} %get-tuple-element.5) | copy-start | bytes 786436

commit v4 on v3

--- a/solution.py
+++ b/solution.py
@@ -265,17 +265,14 @@
         lax.fori_loop(0, 8, body, 0)
 
     def row_last(col, acc, g):
-        mat[...] = jnp.zeros((128, 128), f32)
-
-        def body(q, _):
-            rows = half_rows(q, g)
+        wide = jnp.zeros((128, 128), f32)
+        for q in range(8):
+            rows = slice(q * B + g * 128, q * B + (g + 1) * 128)
             total = acc[rows, :]
             for s in range(NZ):
                 total = total + t_exp[rows, tile(s, 1)] * col[s:s + 1, :]
-            mat[...] = jnp.where(lane == q, jnp.sum(total, axis=1, keepdims=True), mat[...])
-            return 0
-
-        lax.fori_loop(0, 8, body, 0)
+            wide = jnp.where(lane == q, jnp.sum(total, axis=1, keepdims=True), wide)
+        mat[...] = wide
 
     def partition_sum(g):
         mat[...] = jnp.zeros((128, 128), f32)
@@ -287,15 +284,14 @@
 
         lax.fori_loop(0, 8, body, 0)
 
-    def col_part(g, start, tiles):
-        def body(q, acc):
-            rows = half_rows(q, g)
+    def col_part(g, acc, tiles):
+        for q in range(8):
+            rows = slice(q * B + g * 128, q * B + (g + 1) * 128)
             scale = row_b[rows, :]
-            return tuple(
+            acc = tuple(
                 v + jnp.sum((t_exp[rows, at] * scale).reshape(16, 8, 128), axis=0) for v, at in zip(acc, tiles)
             )
-
-        return lax.fori_loop(0, 8, body, start)
+        return acc
 
     def row_to_col(n):
         zeros = jnp.zeros((8, 128), f32)
@@ -402,14 +398,18 @@
 
     us = {}
 
-    def u_pair(j, slots):
+    def u_grad(j, slots):
         grad_part((2 * j + 1) * B, B, slots)
         grad_part(2 * j * B, B, slots)
+
+    def u_pair(j):
         u_send[j] = u_dot(2 * j + 1).astype(bf16)
+        u_ref[j] = u_dot(2 * j)
+
+    def u_start(j):
         cp = copy(u_send.at[j], u_sib.at[j], US, us_rs.at[j], sibling)
         cp.start()
         us[j] = cp
-        u_ref[j] = u_dot(2 * j)
 
     Q = B // NX
     mine = pl.ds(pl.multiple_of(x * Q, Q), Q)
@@ -427,30 +427,38 @@
             at = pl.multiple_of(((x + b) % NX) * Q, Q)
             copy(v_send.at[j, pl.ds(at, Q)], v_recv.at[t], V, vq_rs.at[0], dev(0, j, 0, b)).start()
 
+    rest = (0, 1, 2, 6, 7)
     grad_part(0, ROWS, (3,))
     chunk_dot(3)
+    grad_part(0, ROWS, (5,))
     ring(1, 0)
-    grad_part(0, ROWS, (5,))
     chunk_dot(5)
+    grad_part(0, ROWS, (4,))
     ring(1, 1)
-    grad_part(0, ROWS, (4,))
     chunk_dot(4)
+    u_grad(2, rest)
     ring(0, 0)
     ring(0, 1)
-    rest = (0, 1, 2, 6, 7)
-    u_pair(2, rest)
-    u_pair(1, rest)
+    u_pair(2)
+    u_grad(1, rest)
+    u_start(2)
+    u_pair(1)
+    u_grad(3, rest)
+    u_start(1)
     v_start(2)
-    u_pair(3, rest)
+    u_pair(3)
+    u_grad(0, rest)
+    u_start(3)
     v_start(1)
-    u_pair(0, rest)
+    u_pair(0)
+    u_start(0)
+    v_start(3)
     chunk_dot(2)
     chunk_dot(6)
+    chunk_dot(1)
+    v_start(0)
     ring(2, 0)
     ring(2, 1)
-    v_start(3)
-    v_start(0)
-    chunk_dot(1)
     chunk_dot(7)
     chunk_dot(0)
     ring(3, 0)

time: 88.6 us -> 85.4 us (0.964)
  Pallas kernels: 85.4 us -> 82.2 us
    pallas_call x1, Pallas kernels: 85.4 us -> 82.2 us  [shards(): pl.pallas_call(kernel, out_shape=[jax.ShapeDtypeStruct((B, B), f32), jax....]
where the time goes in v4:
time: 85.4 us; the launch traced here: 85.3 us
  Pallas kernels  82.2 us (96%)
  local copies, waits for them, and re-layouts  2.42 us (3%)
    pallas_call x1, Pallas kernels, shards(): pl.pallas_call(kernel, out_shape=[jax.ShapeDtypeStruct((B, B), f32), jax....  82.2 us
    unnamed x4, local copies, waits for them, and re-layouts  2.42 us

profile of v4, /device:TPU:32, one launch (start us, length us, event | category | flops | bytes accessed | tf_op | source)
XLA Modules:
  0.0 85.3 jit_solution(8200882998363440045)
XLA Ops:
  0.6 82.2 %shard_map.50 = (f32[256,256]{1,0:T(8,128)}, f32[256,256]{1,0:T(8,128)}) custom-call(bf16[256,256]{1,0:T(8,128)(2,1)} %student_ref.1, bf16[256,256]{1,0:T(8,128)(2,1)} %teacher_ref.1, bf16[256,256]{1,0:T(8,128)(2,1)} %proto_ref.1), custom_call_target="tpu_custom_call" | custom-call | tf_op jit(solution)/shard_map/pallas_call | solution.py:508
  82.9 0.0 copy-start
  82.9 1.7 %copy.7 = f32[256,256]{1,0:T(8,128)} copy(f32[256,256]{1,0:T(8,128)} %get-tuple-element.4) | data formatting | bytes 524288
  84.6 0.0 copy-done
  84.6 0.7 copy.8
Async XLA Ops:
  82.9 1.7 %copy-start = (f32[256,256]{1,0:T(8,128)S(1)}, f32[256,256]{1,0:T(8,128)}, u32[]{:S(2)}) copy-start(f32[256,256]{1,0:T(8,128)} %get-tuple-element.5) | copy-start | bytes 786436

commit v5 on v4

--- a/solution.py
+++ b/solution.py
@@ -254,15 +254,12 @@
             out[q * B + g * 128:q * B + (g + 1) * 128, :] = jnp.broadcast_to(wide[:, q:q + 1], (128, 128))
 
     def row_first(col, acc):
-        def body(q, _):
-            rows = pl.ds(pl.multiple_of(q * B, B), B)
+        for r in range(0, ROWS, 128):
+            rows = slice(r, r + 128)
             total = t_exp[rows, tile(0, 0)] * col[0:1, :]
             for s in range(1, NZ):
                 total = total + t_exp[rows, tile(s, 0)] * col[s:s + 1, :]
             acc[rows, :] = total
-            return 0
-
-        lax.fori_loop(0, 8, body, 0)
 
     def row_last(col, acc, g):
         wide = jnp.zeros((128, 128), f32)

time: 85.4 us -> 85.2 us (level)
  no operation moved by 1% of the time
where the time goes in v5:
time: 85.2 us; the launch traced here: 85.1 us
  Pallas kernels  82 us (96%)
  local copies, waits for them, and re-layouts  2.42 us (3%)
    pallas_call x1, Pallas kernels, shards(): pl.pallas_call(kernel, out_shape=[jax.ShapeDtypeStruct((B, B), f32), jax....  82 us
    unnamed x4, local copies, waits for them, and re-layouts  2.42 us

profile of v5, /device:TPU:32, one launch (start us, length us, event | category | flops | bytes accessed | tf_op | source)
XLA Modules:
  0.0 85.1 jit_solution(3571459108433270238)
XLA Ops:
  0.6 82.0 %shard_map.50 = (f32[256,256]{1,0:T(8,128)}, f32[256,256]{1,0:T(8,128)}) custom-call(bf16[256,256]{1,0:T(8,128)(2,1)} %student_ref.1, bf16[256,256]{1,0:T(8,128)(2,1)} %teacher_ref.1, bf16[256,256]{1,0:T(8,128)(2,1)} %proto_ref.1), custom_call_target="tpu_custom_call" | custom-call | tf_op jit(solution)/shard_map/pallas_call | solution.py:505
  82.7 0.0 copy-start
  82.7 1.7 %copy.7 = f32[256,256]{1,0:T(8,128)} copy(f32[256,256]{1,0:T(8,128)} %get-tuple-element.4) | data formatting | bytes 524288
  84.4 0.0 copy-done
  84.4 0.7 copy.8
Async XLA Ops:
  82.7 1.7 %copy-start = (f32[256,256]{1,0:T(8,128)S(1)}, f32[256,256]{1,0:T(8,128)}, u32[]{:S(2)}) copy-start(f32[256,256]{1,0:T(8,128)} %get-tuple-element.5) | copy-start | bytes 786436
